TPU v7x, 256 devices: a whole 4x4x8 slice. The times are simulated.
256 devices in a mesh: node: 16 (over z, core), chip: 16 (over y, x).
Axes of the slice: x: 4, y: 4, z: 8, core: 2. Of those that a mesh axis runs over, the one named last changes fastest.
Arguments:
- x_rows: bfloat16 [49152, 12288], P(('node', 'chip')), may hold values from -6 to 6
- value_cot: bfloat16 [49152, 1024], P(('node', 'chip')), may hold values from -48 to 48
- value_weight: bfloat16 [12288, 1024], P('chip'), may hold values from -0.5 to 0.5
- resp_of_row: int32 [49152], P(('node', 'chip')), may hold values from 0 to 512, as said below
- block_plan: int32 [4096, 3], P(('node', 'chip')), may hold values from -1 to 15, as said below
- resp_len: int32 [512], replicated, may hold values from 1 to 143, as said below
- group_of_resp: int32 [512], replicated, may hold values from 0 to 63, as said below
- rewards: float32 [512], replicated, may hold values from -4 to 4
- send_error: bfloat16 [16, 12288, 1024], P('node', 'chip'), may hold values from -12 to 12
- mean_error: float32 [16, 16, 48, 1024], P('chip', 'node'), may hold values from -6 to 6
Outputs:
- input_grad: bfloat16 [36864, 12288], P(('node', 'chip'))
- new_send_error: bfloat16 [16, 12288, 1024], P('node', 'chip')
- new_mean_error: float32 [16, 16, 48, 1024], P('chip', 'node')
- update: bfloat16 [12288, 1024], P('chip')
Inputs may be any that keep to these rules, and one draw needn't show every extreme that they name: `resp_of_row`: live rows come in whole blocks of 12; each response's rows are consecutive among the live rows of its replica taken in device order; 512 marks a padding row. A device holds between 8 and 16 live blocks. `block_plan`: A live block's receiving chip is in its own replica; every chip receives exactly 12 blocks, one for each place below 12; one device sends at most 1 block to one chip (its send slot is always 0), and some devices send exactly 1 to every chip. A padding block has -1 in all three entries. `resp_len`: the number of rows with that response. `group_of_resp`: every group holds exactly 8 responses.
All inputs are finite; a program needn't handle non-finite values. Where the computation divides by a largest or mean magnitude, that divisor is 1e-20 or more.
Results may differ from a plain program's by a relative error of at most 0.012.
Values may be sent and summed in bfloat16 or wider, within the bound.
A program may use at most 128 MiB of HBM per device.

v0:
```python
import jax
import jax.numpy as jnp
from jax import lax
from jax.sharding import PartitionSpec as P

GSIZE = 8


def squash(running):
    grouped = running.reshape(running.shape[0], running.shape[1] // 128, 128)
    magnitude = jnp.mean(jnp.abs(grouped), axis=2, keepdims=True) + 1e-06
    outgoing = (
        (magnitude * jnp.tanh(grouped / magnitude)).reshape(running.shape).astype(jnp.bfloat16)
    )
    return (outgoing, running - outgoing.astype(jnp.float32))


def contract_rows(first_op, second_op):
    return lax.dot_general(
        first_op, second_op, (((0,), (0,)), ((), ())), preferred_element_type=jnp.float32
    )


def against_weight(cot_rows, weight_rows):
    return lax.dot_general(
        cot_rows, weight_rows, (((1,), (1,)), ((), ())), preferred_element_type=jnp.float32
    )


def select_blocks(labels, wanted):
    label_ids = jnp.arange(labels.shape[0], dtype=jnp.int32)
    matches = labels[None, :] == wanted[:, None]
    chosen = jnp.sum(jnp.where(matches, label_ids[None, :], 0), axis=1)
    present = jnp.any(matches, axis=1)
    return (chosen, present)


def per_device(
    x_rows,
    value_cot,
    value_weight,
    resp_of_row,
    block_plan,
    resp_len,
    group_of_resp,
    rewards,
    send_error,
    mean_error,
):
    chip_count = lax.axis_size("chip")
    node_count = lax.axis_size("node")
    model_width = x_rows.shape[1]
    kv_width = value_cot.shape[1]
    blocks = block_plan.shape[0]
    rows_blk = x_rows.shape[0] // blocks
    live_blocks = 3 * blocks // 4
    work_rows = live_blocks * rows_blk
    piece_cols = model_width // chip_count
    resp_total = rewards.shape[0]
    group_ids = jnp.arange(resp_total // GSIZE, dtype=jnp.int32)
    member = (group_of_resp[:, None] == group_ids[None, :]).astype(jnp.float32)
    group_mean = jnp.sum(member * rewards[:, None], axis=0) / GSIZE
    advantage = rewards - jnp.sum(member * group_mean[None, :], axis=1)
    lookup = advantage / resp_len.astype(jnp.float32)
    resp_ids = jnp.arange(resp_total, dtype=jnp.int32)
    row_weight = jnp.sum(
        jnp.where(resp_of_row[:, None] == resp_ids[None, :], lookup[None, :], 0.0), axis=1
    )
    scaled = (row_weight[:, None] * value_cot.astype(jnp.float32)).astype(jnp.bfloat16)
    pair_slots = max(1, blocks // chip_count)
    send_at = jnp.where(block_plan[:, 0] >= 0, block_plan[:, 0] * pair_slots + block_plan[:, 1], -1)
    chosen, present = select_blocks(send_at, jnp.arange(chip_count * pair_slots, dtype=jnp.int32))
    input_send = jnp.where(
        present[:, None],
        jnp.take(x_rows.reshape(blocks, rows_blk * model_width), chosen, axis=0),
        jnp.zeros((), jnp.bfloat16),
    )
    cot_send = jnp.where(
        present[:, None],
        jnp.take(scaled.reshape(blocks, rows_blk * kv_width), chosen, axis=0),
        jnp.zeros((), jnp.bfloat16),
    )
    place_send = jnp.where(present, jnp.take(block_plan[:, 2], chosen), -1)
    input_recv, cot_recv, place_recv = (
        lax.all_to_all(
            input_send.reshape(chip_count, pair_slots, rows_blk * model_width),
            "chip",
            split_axis=0,
            concat_axis=0,
            tiled=True,
        ),
        lax.all_to_all(
            cot_send.reshape(chip_count, pair_slots, rows_blk * kv_width),
            "chip",
            split_axis=0,
            concat_axis=0,
            tiled=True,
        ),
        lax.all_to_all(
            place_send.reshape(chip_count, pair_slots),
            "chip",
            split_axis=0,
            concat_axis=0,
            tiled=True,
        ),
    )
    chosen, present = select_blocks(
        place_recv.reshape(chip_count * pair_slots), jnp.arange(live_blocks, dtype=jnp.int32)
    )
    packed_input = jnp.take(
        input_recv.reshape(chip_count * pair_slots, rows_blk * model_width), chosen, axis=0
    ).reshape(work_rows, chip_count, piece_cols)
    packed_cot = jnp.take(
        cot_recv.reshape(chip_count * pair_slots, rows_blk * kv_width), chosen, axis=0
    ).reshape(work_rows, kv_width)
    columns = lax.all_to_all(packed_input, "chip", split_axis=1, concat_axis=0, tiled=True).reshape(
        chip_count * work_rows, piece_cols
    )
    shard_rows = lax.all_gather(packed_cot, "chip", axis=0, tiled=True)
    running = contract_rows(columns, shard_rows)
    partial_value = against_weight(shard_rows, value_weight)
    node_grad, partial_value = (running, partial_value)
    input_grad = lax.all_to_all(
        partial_value.astype(jnp.bfloat16), "chip", split_axis=0, concat_axis=1, tiled=True
    )
    outgoing, leftover = squash(node_grad + send_error[0].astype(jnp.float32))
    pieces = outgoing.reshape(node_count, piece_cols // node_count, kv_width)
    arrived = lax.all_to_all(pieces, "node", split_axis=0, concat_axis=0, tiled=True)
    node_mean = jnp.sum(arrived.astype(jnp.float32), axis=0) / node_count
    update_piece, remainder = squash(node_mean + mean_error[0, 0])
    update = lax.all_gather(update_piece, "node", axis=0, tiled=True)
    return (input_grad, leftover.astype(jnp.bfloat16)[None], remainder[None, None], update)


def solution(mesh):
    return jax.shard_map(
        per_device,
        mesh=mesh,
        in_specs=(
            P(("node", "chip"), None),
            P(("node", "chip"), None),
            P("chip", None),
            P(("node", "chip")),
            P(("node", "chip"), None),
            P(),
            P(),
            P(),
            P("node", "chip", None),
            P("chip", "node", None, None),
        ),
        out_specs=(
            P(("node", "chip"), None),
            P("node", "chip", None),
            P("chip", "node", None, None),
            P("chip", None),
        ),
        check_vma=False,
    )
```

profile of v0, /device:TPU:24, one launch (start us, length us, event | category | flops | bytes accessed | tf_op | source)
XLA Modules:
  0.0 396.0 jit_solution(7283657910704080793)
XLA Ops:
  9.6 7.2 %all-to-all-start = ((s32[16,1,1]{2,1,0:T(1,128)}), s32[16,1,1]{2,1,0:T(1,128)S(1)}, u32[]{:S(2)}, u32[]{:S(2)}) async-start(s32[16,1,1]{2,1,0:T(1,128)} %copy.27), calls=%async_computation | async-start | bytes 16384 | tf_op jit(solution)/shard_map/all_to_all | solution.py:99
  16.8 10.3 %reshape.276 = bf16[16,147456]{1,0:T(8,128)(2,1)} reshape(bf16[192,12288]{1,0:T(8,128)(2,1)} %param.10) | data formatting | bytes 9437184 | tf_op jit(solution)/shard_map/reshape | solution.py:75
  27.1 4.9 %fusion.14 = (bf16[16,73728]{1,0:T(8,128)(2,1)}, bf16[16,73728]{1,0:T(8,128)(2,1)}) fusion(bf16[16,147456]{1,0:T(8,128)(2,1)} %reshape.276), kind=kLoop, calls=%fused_computation.70 | loop fusion | bytes 9437184 | tf_op jit(solution)/shard_map/jit(_take)/gather | solution.py:75
  32.0 7.5 %gather_fusion.3 = bf16[16,73728]{1,0:T(8,128)(2,1)} fusion(bf16[16,73728]{1,0:T(8,128)(2,1)} %get-tuple-element.8, s32[1024]{0:T(1024)S(1)} %pad_clamp_fusion.1), kind=kCustom, calls=%fused_computation.3 | custom fusion | bytes 4718656 | tf_op jit(solution)/shard_map/jit(_take)/gather | solution.py:75
  39.5 7.5 %gather_fusion.4 = bf16[16,73728]{1,0:T(8,128)(2,1)} fusion(bf16[16,73728]{1,0:T(8,128)(2,1)} %get-tuple-element.9, s32[1024]{0:T(1024)S(1)} %pad_clamp_fusion.1), kind=kCustom, calls=%fused_computation.4 | custom fusion | bytes 4718656 | tf_op jit(solution)/shard_map/jit(_take)/gather | solution.py:75
  51.5 7.5 %all-to-all-start.1 = ((bf16[16,2,6144]{2,1,0:T(2,128)(2,1)}), bf16[16,2,6144]{2,1,0:T(2,128)(2,1)S(1)}, u32[]{:S(2)}, u32[]{:S(2)}) async-start(bf16[16,2,6144]{2,1,0:T(2,128)(2,1)} %reshape.338), calls=%async_computation.1 | async-start | bytes 786432 | tf_op jit(solution)/shard_map/all_to_all | solution.py:92
  59.0 6.0 %fusion.1 = bf16[16,1,147456]{2,0,1:T(8,128)(2,1)} fusion(bf16[16,73728]{1,0:T(8,128)(2,1)} %gather_fusion.4, bf16[16,73728]{1,0:T(8,128)(2,1)} %gather_fusion.3, pred[16]{0:T(512)(128)(4,1)S(1)} %compare_and_fusion, pred[16]{0:T(512)(128)(4,1)S(1)} %fusion.8), kind=kLoop, calls=%fused_computation.10 | loop fusion | flops 14155776 | bytes 9437216 | tf_op jit(solution)/shard_map/jit(_where)/select_n | solution.py:73
  65.0 6.8 %reduce.2 = bf16[16,147456]{1,0:T(8,128)(2,1)} reduce(bf16[16,1,147456]{2,0,1:T(8,128)(2,1)} %fusion.1, bf16[]{:T(256)} %broadcast.339), dimensions={1}, to_apply=%copy.30.reduce_sub_computation | reduce | bytes 9437186 | tf_op jit(solution)/shard_map/jit(_where)/select_n | solution.py:73
  71.8 7.3 %reshape.340 = bf16[16,2,73728]{2,1,0:T(2,128)(2,1)} reshape(bf16[16,147456]{1,0:T(8,128)(2,1)} %reduce.2) | data formatting | bytes 9437184
  79.1 7.2 %all-to-all-start.3 = ((bf16[16,2,73728]{2,1,0:T(2,128)(2,1)}), bf16[16,2,73728]{2,1,0:T(2,128)(2,1)}, u32[]{:S(2)}, u32[]{:S(2)}) async-start(bf16[16,2,73728]{2,1,0:T(2,128)(2,1)} %reshape.340), calls=%async_computation.3 | async-start | bytes 9437184 | tf_op jit(solution)/shard_map/all_to_all | solution.py:85
  90.0 66.6 %all-to-all-done.3 = bf16[16,2,73728]{2,1,0:T(2,128)(2,1)} async-done(((bf16[16,2,73728]{2,1,0:T(2,128)(2,1)}), bf16[16,2,73728]{2,1,0:T(2,128)(2,1)}, u32[]{:S(2)}, u32[]{:S(2)}) %all-to-all-start.3) | async-done | bytes 4718624 | tf_op jit(solution)/shard_map/all_to_all | solution.py:85
  156.6 12.9 %reshape.341 = bf16[16,1,147456]{2,1,0:T(2,128)(2,1)} reshape(bf16[16,2,73728]{2,1,0:T(2,128)(2,1)} %all-to-all-done.3) | data formatting | bytes 9437184
  169.5 10.2 %copy.46 = bf16[16,1,147456]{2,0,1:T(8,128)(2,1)S(1)} copy(bf16[16,1,147456]{2,1,0:T(2,128)(2,1)} %reshape.341) | data formatting | bytes 9437184
  182.2 6.6 %gather_fusion.5 = bf16[12,73728]{1,0:T(8,128)(2,1)} fusion(bf16[16,73728]{1,0:T(8,128)(2,1)} %get-tuple-element.6, s32[1024]{0:T(1024)S(1)} %pad_clamp_fusion), kind=kCustom, calls=%fused_computation.5 | custom fusion | bytes 3538992 | tf_op jit(solution)/shard_map/jit(_take)/gather | solution.py:110
  188.8 6.6 %gather_fusion.6 = bf16[12,73728]{1,0:T(8,128)(2,1)} fusion(bf16[16,73728]{1,0:T(8,128)(2,1)} %get-tuple-element.7, s32[1024]{0:T(1024)S(1)} %pad_clamp_fusion), kind=kCustom, calls=%fused_computation.6 | custom fusion | bytes 3538992 | tf_op jit(solution)/shard_map/jit(_take)/gather | solution.py:110
  195.4 5.7 %pad_maximum_fusion = bf16[12,147456]{1,0:T(8,128)(2,1)} fusion(bf16[12,73728]{1,0:T(8,128)(2,1)} %gather_fusion.6, bf16[12,73728]{1,0:T(8,128)(2,1)} %gather_fusion.5), kind=kLoop, calls=%fused_computation.11 | loop fusion | flops 7077888 | bytes 7077888
  201.1 5.7 %gather.39 = bf16[144,16,768]{2,1,0:T(8,128)(2,1)} reshape(bf16[12,147456]{1,0:T(8,128)(2,1)} %pad_maximum_fusion) | data formatting | bytes 7077888 | tf_op jit(solution)/shard_map/jit(_take)/gather | solution.py:110
  211.1 44.1 %all_to_all.55 = bf16[144,16,768]{2,0,1:T(8,128)(2,1)} all-to-all(bf16[144,16,768]{2,0,1:T(8,128)(2,1)S(1)} %copy_select_fusion), channel_id=1, replica_groups=mesh['node'=16,'chip'=16] {'chip'}, dimensions={1} | all-to-all | bytes 7077888 | tf_op jit(solution)/shard_map/all_to_all | solution.py:116
  255.2 6.8 %convert_add_fusion = f32[768,1024]{1,0:T(8,128)S(1)} fusion(bf16[2304,768]{1,0:T(8,128)(2,1)} %bitcast.101, bf16[2304,1024]{1,0:T(8,128)(2,1)} %all-gather.3.cloned.1.call-done, bf16[1,768,1024]{2,1,0:T(8,128)(2,1)S(1)} %copy-done.9), kind=kOutput, calls=%fused_computation.18 | convolution fusion | flops 3625451520 | bytes 12976128 | tf_op jit(solution)/shard_map/dot_general | solution.py:19
  273.9 8.4 %all-to-all-start.5 = ((bf16[16,48,1024]{2,1,0:T(8,128)(2,1)}), bf16[16,48,1024]{2,1,0:T(8,128)(2,1)S(1)}, u32[]{:S(2)}, u32[]{:S(2)}) async-start(bf16[16,48,1024]{2,1,0:T(8,128)(2,1)} %bitcast.98), calls=%async_computation.5 | async-start | bytes 3145728 | tf_op jit(solution)/shard_map/all_to_all | solution.py:128
  283.1 7.7 %convolution_convert_fusion = bf16[2304,768]{1,0:T(8,128)(2,1)} fusion(bf16[2304,1024]{1,0:T(8,128)(2,1)} %all-gather.3.cloned.1.call-done, bf16[768,1024]{1,0:T(8,128)(2,1)S(1)} %copy-done), kind=kOutput, calls=%fused_computation.7 | convolution fusion | flops 3625648128 | bytes 9830400 | tf_op jit(solution)/shard_map/dot_general | solution.py:25
  290.8 29.5 %all-to-all-done.5 = bf16[16,48,1024]{2,1,0:T(8,128)(2,1)S(1)} async-done(((bf16[16,48,1024]{2,1,0:T(8,128)(2,1)}), bf16[16,48,1024]{2,1,0:T(8,128)(2,1)S(1)}, u32[]{:S(2)}, u32[]{:S(2)}) %all-to-all-start.5) | async-done | bytes 1572896 | tf_op jit(solution)/shard_map/all_to_all | solution.py:128
  320.2 6.7 %all-to-all-start.2 = ((bf16[16,144,768]{2,1,0:T(8,128)(2,1)}), bf16[16,144,768]{2,1,0:T(8,128)(2,1)}, u32[]{:S(2)}, u32[]{:S(2)}) async-start(bf16[16,144,768]{2,1,0:T(8,128)(2,1)} %bitcast.99), calls=%async_computation.2 | async-start | bytes 7077888 | tf_op jit(solution)/shard_map/all_to_all | solution.py:123
  330.0 52.1 %all-to-all-done.2 = bf16[16,144,768]{2,1,0:T(8,128)(2,1)} async-done(((bf16[16,144,768]{2,1,0:T(8,128)(2,1)}), bf16[16,144,768]{2,1,0:T(8,128)(2,1)}, u32[]{:S(2)}, u32[]{:S(2)}) %all-to-all-start.2) | async-done | bytes 3538976 | tf_op jit(solution)/shard_map/all_to_all | solution.py:123
  (82 shorter events, 39.9 us)
Async XLA Ops:
  7.2 275.9 %copy-start = (bf16[768,1024]{1,0:T(8,128)(2,1)S(1)}, bf16[768,1024]{1,0:T(8,128)(2,1)}, u32[]{:S(2)}) copy-start(bf16[768,1024]{1,0:T(8,128)(2,1)} %param.12) | copy-start | bytes 4718596
  9.6 41.8 %all-to-all-start = ((s32[16,1,1]{2,1,0:T(1,128)}), s32[16,1,1]{2,1,0:T(1,128)S(1)}, u32[]{:S(2)}, u32[]{:S(2)}) async-start(s32[16,1,1]{2,1,0:T(1,128)} %copy.27), calls=%async_computation | async-start | bytes 16384 | tf_op jit(solution)/shard_map/all_to_all | solution.py:99
  39.4 7.5 %copy-start.5 = (s32[512]{0:T(512)S(1)}, s32[512]{0:T(512)}, u32[]{:S(2)}) copy-start(s32[512]{0:T(512)} %param.16) | copy-start | bytes 6148
  39.4 7.5 %copy-start.6 = (f32[512]{0:T(512)S(1)}, f32[512]{0:T(512)}, u32[]{:S(2)}) copy-start(f32[512]{0:T(512)} %param.17) | copy-start | bytes 6148
  39.4 7.7 %copy-start.7 = (s32[512]{0:T(512)S(1)}, s32[512]{0:T(512)}, u32[]{:S(2)}) copy-start(s32[512]{0:T(512)} %param.15) | copy-start | bytes 6148
  39.4 7.7 %copy-start.8 = (s32[192]{0:T(256)S(1)}, s32[192]{0:T(256)}, u32[]{:S(2)}) copy-start(s32[192]{0:T(256)} %param.13) | copy-start | bytes 2308
  39.4 7.9 %copy-start.4 = (bf16[192,1024]{1,0:T(8,128)(2,1)S(1)}, bf16[192,1024]{1,0:T(8,128)(2,1)}, u32[]{:S(2)}) copy-start(bf16[192,1024]{1,0:T(8,128)(2,1)} %param.11) | copy-start | bytes 1179652
  51.5 27.6 %all-to-all-start.1 = ((bf16[16,2,6144]{2,1,0:T(2,128)(2,1)}), bf16[16,2,6144]{2,1,0:T(2,128)(2,1)S(1)}, u32[]{:S(2)}, u32[]{:S(2)}) async-start(bf16[16,2,6144]{2,1,0:T(2,128)(2,1)} %reshape.338), calls=%async_computation.1 | async-start | bytes 786432 | tf_op jit(solution)/shard_map/all_to_all | solution.py:92
  79.1 77.5 %all-to-all-start.3 = ((bf16[16,2,73728]{2,1,0:T(2,128)(2,1)}), bf16[16,2,73728]{2,1,0:T(2,128)(2,1)}, u32[]{:S(2)}, u32[]{:S(2)}) async-start(bf16[16,2,73728]{2,1,0:T(2,128)(2,1)} %reshape.340), calls=%async_computation.3 | async-start | bytes 9437184 | tf_op jit(solution)/shard_map/all_to_all | solution.py:85
  86.3 168.9 %all-gather.3.cloned.1.call-start = ((), (), s32[]{:S(2)}) async-start(), calls=%async_computation.6 | async-start | bytes 5013504 | tf_op jit(solution)/shard_map/all_gather | solution.py:119
  211.1 44.1 %copy-start.9 = (bf16[1,768,1024]{2,1,0:T(8,128)(2,1)S(1)}, bf16[1,768,1024]{2,1,0:T(8,128)(2,1)}, u32[]{:S(2)}) copy-start(bf16[1,768,1024]{2,1,0:T(8,128)(2,1)} %param.18) | copy-start | bytes 4718596
  262.0 1.7 copy-start.1
  268.9 1.9 copy-start.2
  273.9 8.4 %copy-start.3 = (f32[1,1,48,1024]{3,2,1,0:T(8,128)S(1)}, f32[1,1,48,1024]{3,2,1,0:T(8,128)}, u32[]{:S(2)}) copy-start(f32[1,1,48,1024]{3,2,1,0:T(8,128)} %param.19) | copy-start | bytes 589828
  273.9 46.3 %all-to-all-start.5 = ((bf16[16,48,1024]{2,1,0:T(8,128)(2,1)}), bf16[16,48,1024]{2,1,0:T(8,128)(2,1)S(1)}, u32[]{:S(2)}, u32[]{:S(2)}) async-start(bf16[16,48,1024]{2,1,0:T(8,128)(2,1)} %bitcast.98), calls=%async_computation.5 | async-start | bytes 3145728 | tf_op jit(solution)/shard_map/all_to_all | solution.py:128
  320.2 61.9 %all-to-all-start.2 = ((bf16[16,144,768]{2,1,0:T(8,128)(2,1)}), bf16[16,144,768]{2,1,0:T(8,128)(2,1)}, u32[]{:S(2)}, u32[]{:S(2)}) async-start(bf16[16,144,768]{2,1,0:T(8,128)(2,1)} %bitcast.99), calls=%async_computation.2 | async-start | bytes 7077888 | tf_op jit(solution)/shard_map/all_to_all | solution.py:123
  326.9 59.4 %all-gather.5.cloned.1.call-start = ((), (), s32[]{:S(2)}) async-start(), calls=%async_computation.7 | async-start | bytes 1671168 | tf_op jit(solution)/shard_map/all_gather | solution.py:131
Sparse Core Ops, SparseCore 0:
  90.2 91.8 all-gather.2
  330.2 38.0 all-gather.4
where the time goes:
time: 404 us; the launch traced here: 396 us
  waiting for transfers between devices  148 us (37%)
  local copies, waits for them, and re-layouts  102 us (25%)
  blocking collectives  44.1 us (11%)
  starting transfers between devices  37.1 us (9%)
  other arithmetic  36 us (9%)
  between operations  14.6 us (4%)
  matrix products  14.5 us (4%)
    all_to_all x1, waiting for transfers between devices, per_device(): lax.all_to_all(input_send.reshape(chip_count, pair_slots, rows_blk * mode...  66.6 us
    all_to_all x1, waiting for transfers between devices, per_device(): lax.all_to_all(partial_value.astype(jnp.bfloat16), 'chip', split_axis=0,...  52.1 us
    all_to_all x1, blocking collectives, per_device(): lax.all_to_all(packed_input, 'chip', split_axis=1, concat_axis=0, tiled=T...  44.1 us
    unnamed x30, local copies, waits for them, and re-layouts  40.3 us
    all_to_all x1, waiting for transfers between devices, per_device(): lax.all_to_all(pieces, 'node', split_axis=0, concat_axis=0, tiled=True)  29.5 us
    gather x4, local copies, waits for them, and re-layouts, per_device(): jnp.take(input_recv.reshape(chip_count * pair_slots, rows_blk * model_wid...  21.4 us
    gather x3, local copies, waits for them, and re-layouts, per_device(): jnp.take(x_rows.reshape(blocks, rows_blk * model_width), chosen, axis=0)  19.8 us
    select_n x2, other arithmetic, per_device(): jnp.where(present[:, None], jnp.take(x_rows.reshape(blocks, rows_blk * mo...  12.8 us
  transfers between devices with their start and end apart: 7, of which 3 were waited for; matrix products, arithmetic and copies ran while one was open for 32% of the time, Pallas kernels for 0%

commit v1 on v0

v1 whole, which is shorter than its diff:
```python
import functools

import jax
import jax.numpy as jnp
from jax import lax
from jax.experimental import pallas as pl
from jax.experimental.pallas import tpu as pltpu
from jax.sharding import PartitionSpec as P

MESH = pl.DeviceIdType.MESH
GSIZE = 8
SIDE = 4
CHIPS = 16
BLK = 12
NBLK = 16
SLOT = 192
WORK = 144
KV = 1024
COLS = 768
PIECE = 48
DEPTH = 8

GROUPS = (
    ((1, 0), (3, 0), (0, 1), (0, 3)),
    ((2, 0), (0, 2)),
    ((1, 1), (3, 3)),
    ((1, 3), (3, 1)),
    ((2, 2),),
    ((1, 2), (3, 2), (2, 1), (2, 3)),
)
ALL = tuple(o for group in GROUPS for o in group)
Z_ORDER = (4, 3, 5, 2, 6, 1, 7)


def squash(e):
    sent, left = [], []
    for j in range(KV // 128):
        g = e[:, 128 * j : 128 * (j + 1)]
        m = jnp.mean(jnp.abs(g), axis=1, keepdims=True) + 1e-06
        s = (m * jnp.tanh(g * (1.0 / m))).astype(jnp.bfloat16)
        sent.append(s)
        left.append(g - s.astype(jnp.float32))
    return sent, left


def row_weights(resp, rlen, grp, rew):
    resp_total = rew.shape[1]
    groups = resp_total // GSIZE
    member = lax.broadcasted_iota(jnp.int32, (groups, resp_total), 0) == grp
    mean = jnp.sum(jnp.where(member, rew, 0.0), axis=1, keepdims=True) / GSIZE
    advantage = rew - jnp.sum(jnp.where(member, mean, 0.0), axis=0, keepdims=True)
    lookup = advantage / rlen.astype(jnp.float32)
    ids = lax.broadcasted_iota(jnp.int32, (SLOT, resp_total), 1)
    return jnp.sum(jnp.where(resp == ids, lookup, 0.0), axis=1, keepdims=True)


def kernel(
    x_hbm, cot_hbm, w_hbm, resp_ref, plan_ref, rlen_ref, grp_ref, rew_ref, serr_hbm, merr_hbm,
    ig_out, nse_out, nme_out, upd_out,
    cot, w, serr, merr, cbuf, cf, xr, stage, gbuf, acc, sbuf, sib, zs, zr, pbuf, chv, chs,
    lsem, csend, crecv, xsend, xrecv, psend, precv, gsend, grecv,
    ssend, srecv, zsend, zrecv, usend, urecv, fsend, frecv,
):
    node, chip = lax.axis_index("node"), lax.axis_index("chip")
    y, x = chip // SIDE, lax.rem(chip, SIDE)
    z, core = node // 2, lax.rem(node, 2)
    other = 1 - core

    def plane(dx, dy):
        return lax.rem(y + dy, SIDE) * SIDE + lax.rem(x + dx, SIDE)

    def deep(dz):
        return lax.rem(z + dz, DEPTH)

    def remote(src, dst, send, recv, node_to, chip_to):
        return pltpu.make_async_remote_copy(
            src_ref=src, dst_ref=dst, send_sem=send, recv_sem=recv,
            device_id=(node_to, chip_to), device_id_type=MESH,
        )

    barrier = pltpu.get_barrier_semaphore()
    for dx, dy in ALL:
        pl.semaphore_signal(barrier, 1, device_id=(node, plane(dx, dy)), device_id_type=MESH)
    for dz in Z_ORDER:
        pl.semaphore_signal(barrier, 1, device_id=(deep(dz) * 2 + core, chip), device_id_type=MESH)
    pl.semaphore_signal(barrier, 1, device_id=(z * 2 + other, chip), device_id_type=MESH)

    loads = [
        pltpu.make_async_copy(cot_hbm, cot, lsem.at[0]),
        pltpu.make_async_copy(w_hbm, w, lsem.at[1]),
        pltpu.make_async_copy(serr_hbm, serr, lsem.at[2]),
        pltpu.make_async_copy(merr_hbm, merr, lsem.at[3]),
        pltpu.make_async_copy(
            x_hbm.at[:, pl.ds(pl.multiple_of(chip * COLS, 128), COLS)], xr.at[chip], lsem.at[4]
        ),
    ]
    for load in loads:
        load.start()

    weight = row_weights(resp_ref[...], rlen_ref[...], grp_ref[...], rew_ref[...])
    goes = plan_ref[...]
    target = jnp.where(goes[:, 0:1] >= 0, goes[:, 0:1] * (WORK // BLK) + goes[:, 2:3], -1)
    pbuf[chip] = jnp.broadcast_to(target, (NBLK, 128))
    loads[0].wait()
    cbuf[y, x] = (weight * cot[...].astype(jnp.float32)).astype(jnp.bfloat16)

    pl.semaphore_wait(barrier, len(ALL) + len(Z_ORDER) + 1)

    xp, xm = lax.rem(x + 1, SIDE), lax.rem(x + 3, SIDE)
    yp, ym = lax.rem(y + 1, SIDE), lax.rem(y + 3, SIDE)
    half, quarter = SLOT // 2, SLOT // 4

    def hop(i, block, to_y, to_x):
        return remote(block, block, csend.at[i], crecv.at[i], node, to_y * SIDE + to_x)

    lo, hi = pl.ds(0, half), pl.ds(half, half)
    q0, q1, q2, q3 = (pl.ds(quarter * i, quarter) for i in range(4))
    c = [
        hop(0, cbuf.at[y, x, lo], y, xp),
        hop(1, cbuf.at[y, x, lo], y, xm),
        hop(2, cbuf.at[y, x, hi], yp, x),
        hop(3, cbuf.at[y, x, hi], ym, x),
        hop(4, cbuf.at[y, xm, q0], y, xp),
        hop(5, cbuf.at[y, xp, q1], y, xm),
        hop(6, cbuf.at[ym, x, q2], yp, x),
        hop(7, cbuf.at[yp, x, q3], ym, x),
        hop(8, cbuf.at[y, :, lo], yp, x),
        hop(9, cbuf.at[y, :, lo], ym, x),
        hop(10, cbuf.at[:, x, hi], y, xp),
        hop(11, cbuf.at[:, x, hi], y, xm),
        hop(12, cbuf.at[ym, :, q0], yp, x),
        hop(13, cbuf.at[yp, :, q1], ym, x),
        hop(14, cbuf.at[:, xm, q2], y, xp),
        hop(15, cbuf.at[:, xp, q3], y, xm),
    ]

    def columns(dx, dy):
        to = plane(dx, dy)
        i = dy * SIDE + dx
        return remote(
            x_hbm.at[:, pl.ds(pl.multiple_of(to * COLS, 128), COLS)], xr.at[chip],
            xsend.at[i], xrecv.at[i], node, to,
        )

    def plans(dx, dy):
        i = dy * SIDE + dx
        return remote(pbuf.at[chip], pbuf.at[chip], psend.at[i], precv.at[i], node, plane(dx, dy))

    xs = {o: columns(*o) for o in ALL}
    ps = [plans(*o) for o in ALL]

    for i in (0, 1, 2, 3):
        c[i].start()
    for p in ps:
        p.start()
    for o in GROUPS[0]:
        xs[o].start()
    for i in (0, 1, 2, 3):
        c[i].wait_recv()
        c[i + 4].start()
    for i in (4, 5):
        c[i].wait_recv()
    c[8].start()
    c[9].start()
    for i in (6, 7):
        c[i].wait_recv()
    c[10].start()
    c[11].start()
    for o in GROUPS[1] + GROUPS[2]:
        xs[o].start()
    for i in (8, 9, 10, 11):
        c[i].wait_recv()
        c[i + 4].start()
    for o in GROUPS[3] + GROUPS[4] + GROUPS[5]:
        xs[o].start()

    for p in ps:
        p.wait_recv()
    where = pbuf[...].reshape(CHIPS * NBLK, 128)
    block = lax.broadcasted_iota(jnp.int32, (CHIPS * NBLK, 128), 0)
    lane = lax.broadcasted_iota(jnp.int32, (CHIPS * NBLK, 128), 1)
    chv[:, 0:128] = jnp.max(jnp.where(where == lane, block, 0), axis=0, keepdims=True)
    chv[:, 128:256] = jnp.max(jnp.where(where == lane + 128, block, 0), axis=0, keepdims=True)
    choose = pltpu.make_async_copy(chv, chs, lsem.at[5])
    choose.start()
    choose.wait()

    for i in (12, 13, 14, 15):
        c[i].wait_recv()
    loads[1].wait()

    def widen(s, carry):
        rows = cbuf[s // SIDE, lax.rem(s, SIDE)].astype(jnp.float32)
        for j in range(NBLK):
            cf[s * NBLK + j] = rows[j * BLK : (j + 1) * BLK]
        return carry

    lax.fori_loop(0, CHIPS, widen, 0)

    two = 2 * WORK // BLK

    def input_grad(s, carry):
        for j in range(two):
            b = chs[0, s * two + j]
            stage[pl.ds(j * BLK, BLK), :] = cf[b]
        rows = lax.dot_general(
            stage[...].astype(jnp.bfloat16), w[...], (((1,), (1,)), ((), ())),
            preferred_element_type=jnp.float32,
        )
        gbuf[pl.ds(2 * s, 2)] = rows.astype(jnp.bfloat16).reshape(2, WORK, COLS)
        return carry

    lax.fori_loop(0, CHIPS // 2, input_grad, 0)

    def owners(dx, dy):
        to = plane(dx, dy)
        i = dy * SIDE + dx
        return remote(
            gbuf.at[to], ig_out.at[:, pl.ds(pl.multiple_of(chip * COLS, 128), COLS)],
            gsend.at[i], grecv.at[i], node, to,
        )

    own_grad = pltpu.make_async_copy(
        gbuf.at[chip], ig_out.at[:, pl.ds(pl.multiple_of(chip * COLS, 128), COLS)], lsem.at[6]
    )
    own_grad.start()
    for o in ALL:
        xs[o].wait_send()
    gs = [owners(*o) for o in ALL]
    for g in gs:
        g.start()

    loads[4].wait()
    for o in ALL:
        xs[o].wait_recv()
    acc[...] = jnp.zeros_like(acc)

    def contract(s, carry):
        acc[...] += lax.dot_general(
            xr[pl.ds(s * SIDE, SIDE)].reshape(SIDE * SLOT, COLS), cbuf[s].reshape(SIDE * SLOT, KV),
            (((0,), (0,)), ((), ())), preferred_element_type=jnp.float32,
        )
        return carry

    lax.fori_loop(0, SIDE, contract, 0)

    loads[2].wait()

    def compress(which):
        def one(k, carry):
            p = pl.multiple_of((k * 2 + which) * PIECE, PIECE)
            e = acc[pl.ds(p, PIECE), :] + serr[pl.ds(p, PIECE), :].astype(jnp.float32)
            sent, left = squash(e)
            for j in range(KV // 128):
                sbuf[which, k, :, 128 * j : 128 * (j + 1)] = sent[j]
                nse_out[pl.ds(p, PIECE), 128 * j : 128 * (j + 1)] = left[j].astype(jnp.bfloat16)
            return carry

        lax.fori_loop(0, DEPTH, one, 0)

    compress(other)
    pair = remote(sbuf.at[other], sib, ssend, srecv, z * 2 + other, chip)
    pair.start()
    compress(core)
    pair.wait_recv()

    zc = {}
    for dz in Z_ORDER:
        to = deep(dz)
        zs[to] = (sbuf[core, to].astype(jnp.float32) + sib[to].astype(jnp.float32)).astype(jnp.bfloat16)
        zc[dz] = remote(zs.at[to], zr.at[dz], zsend.at[dz], zrecv.at[dz], to * 2 + core, chip)
        zc[dz].start()
    total = sbuf[core, z].astype(jnp.float32) + sib[z].astype(jnp.float32)
    for dz in reversed(Z_ORDER):
        zc[dz].wait_recv()
        total = total + zr[dz].astype(jnp.float32)
    loads[3].wait()
    sent, left = squash(total * (1.0 / 16) + merr[...])
    for j in range(KV // 128):
        upd_out[node, :, 128 * j : 128 * (j + 1)] = sent[j]
        nme_out[:, 128 * j : 128 * (j + 1)] = left[j]

    us = {}
    for dz in Z_ORDER:
        us[dz] = remote(
            upd_out.at[node], upd_out.at[node], usend.at[dz], urecv.at[dz], deep(dz) * 2 + core, chip
        )
        us[dz].start()
    fs = []

    def share(i, n):
        f = remote(upd_out.at[n], upd_out.at[n], fsend.at[i], frecv.at[i], z * 2 + other, chip)
        f.start()
        fs.append(f)

    share(0, node)
    for dz in reversed(Z_ORDER):
        us[dz].wait_recv()
        share(dz, deep(DEPTH - dz) * 2 + core)
    for f in fs:
        f.wait_recv()
    own_grad.wait()
    for g in gs:
        g.wait_recv()
    for s in c + ps + gs + fs + [pair] + list(zc.values()) + list(us.values()):
        s.wait_send()


def per_device(
    x_rows, value_cot, value_weight, resp_of_row, block_plan, resp_len, group_of_resp, rewards, send_error, mean_error
):
    vmem = pl.BlockSpec(memory_space=pltpu.VMEM)
    hbm = pl.BlockSpec(memory_space=pl.ANY)
    bf16, f32, i32 = jnp.bfloat16, jnp.float32, jnp.int32
    dma = pltpu.SemaphoreType.DMA
    ig, nse, nme, upd = pl.pallas_call(
        kernel,
        out_shape=(
            jax.ShapeDtypeStruct((WORK, CHIPS * COLS), bf16),
            jax.ShapeDtypeStruct((COLS, KV), bf16),
            jax.ShapeDtypeStruct((PIECE, KV), f32),
            jax.ShapeDtypeStruct((CHIPS, PIECE, KV), bf16),
        ),
        in_specs=[hbm, hbm, hbm, vmem, vmem, vmem, vmem, vmem, hbm, hbm],
        out_specs=(hbm, vmem, vmem, vmem),
        scratch_shapes=[
            pltpu.VMEM((SLOT, KV), bf16),
            pltpu.VMEM((COLS, KV), bf16),
            pltpu.VMEM((COLS, KV), bf16),
            pltpu.VMEM((PIECE, KV), f32),
            pltpu.VMEM((SIDE, SIDE, SLOT, KV), bf16),
            pltpu.VMEM((CHIPS * NBLK, BLK, KV), f32),
            pltpu.VMEM((CHIPS, SLOT, COLS), bf16),
            pltpu.VMEM((2 * WORK, KV), f32),
            pltpu.VMEM((CHIPS, WORK, COLS), bf16),
            pltpu.VMEM((COLS, KV), f32),
            pltpu.VMEM((2, DEPTH, PIECE, KV), bf16),
            pltpu.VMEM((DEPTH, PIECE, KV), bf16),
            pltpu.VMEM((DEPTH, PIECE, KV), bf16),
            pltpu.VMEM((DEPTH, PIECE, KV), bf16),
            pltpu.VMEM((CHIPS, NBLK, 128), i32),
            pltpu.VMEM((1, 256), i32),
            pltpu.SMEM((1, 256), i32),
            dma((8,)), dma((16,)), dma((16,)), dma((16,)), dma((16,)), dma((16,)), dma((16,)),
            dma((16,)), dma((16,)), dma, dma, dma((8,)), dma((8,)), dma((8,)), dma((8,)),
            dma((8,)), dma((8,)),
        ],
        compiler_params=pltpu.CompilerParams(
            collective_id=0, has_side_effects=True, vmem_limit_bytes=58 * 2**20
        ),
        cost_estimate=pl.CostEstimate(flops=8_000_000_000, bytes_accessed=20_000_000, transcendentals=800_000),
    )(
        x_rows, value_cot, value_weight, resp_of_row.reshape(SLOT, 1), block_plan,
        resp_len.reshape(1, -1), group_of_resp.reshape(1, -1), rewards.reshape(1, -1),
        send_error.reshape(COLS, KV), mean_error.reshape(PIECE, KV),
    )
    return ig, nse[None], nme[None, None], upd.reshape(COLS, KV)


def solution(mesh):
    return jax.shard_map(
        per_device,
        mesh=mesh,
        in_specs=(
            P(("node", "chip"), None),
            P(("node", "chip"), None),
            P("chip", None),
            P(("node", "chip")),
            P(("node", "chip"), None),
            P(),
            P(),
            P(),
            P("node", "chip", None),
            P("chip", "node", None, None),
        ),
        out_specs=(
            P(("node", "chip"), None),
            P("node", "chip", None),
            P("chip", "node", None, None),
            P("chip", None),
        ),
        check_vma=False,
    )
```

time: 404 us -> 171 us (0.42); the launches traced: 396 us -> 169 us
  Pallas kernels: 0 us -> 158 us
  waiting for transfers between devices: 148 us -> 0 us
  local copies, waits for them, and re-layouts: 102 us -> 10.2 us
  blocking collectives: 44.1 us -> 0 us
  starting transfers between devices: 37.1 us -> 0 us
  other arithmetic: 36 us -> 0 us
  matrix products: 14.5 us -> 0 us
  between operations: 14.6 us -> 0.65 us
    pallas_call x0 -> x1, Pallas kernels: none -> 158 us  [per_device(): pl.pallas_call(kernel, out_shape=(jax.ShapeDtypeStruct((WORK, CHIPS * COL...]
    all_to_all x5 -> x0, waiting for transfers between devices: 148 us -> none  [the longest x1 66.6 us: per_device(): lax.all_to_all(input_send.reshape(chip_count, pair_slots, rows_blk * mode...]
    all_to_all x1 -> x0, blocking collectives: 44.1 us -> none  [per_device(): lax.all_to_all(packed_input, 'chip', split_axis=1, concat_axis=0, tiled=T...]
    gather x11 -> x0, local copies, waits for them, and re-layouts: 43.9 us -> none  [the longest x4 21.4 us: per_device(): jnp.take(input_recv.reshape(chip_count * pair_slots, rows_blk * model_wid...]
    all_to_all x5 -> x0, starting transfers between devices: 37 us -> none  [the longest x1 8.42 us: per_device(): lax.all_to_all(pieces, 'node', split_axis=0, concat_axis=0, tiled=True)]
    unnamed x30 -> x11, local copies, waits for them, and re-layouts: 40.3 us -> 8.81 us
    select_n x9 -> x0, other arithmetic: 18.9 us -> none  [the longest x2 12.8 us: per_device(): jnp.where(present[:, None], jnp.take(x_rows.reshape(blocks, rows_blk * mo...]
    dot_general x2 -> x0, matrix products: 14.5 us -> none  [the longest x1 7.67 us: against_weight(): lax.dot_general(cot_rows, weight_rows, (((1,), (1,)), ((), ())), preferre...]
  transfers between devices with their start and end apart: 7 -> 0, of which waited for: 3 -> 0; matrix products, arithmetic and copies ran while one was open for 32% -> 0% of each run, Pallas kernels for 0% -> 0%
where the time goes in v1:
time: 171 us; the launch traced here: 169 us
  Pallas kernels  158 us (92%)
  local copies, waits for them, and re-layouts  10.2 us (6%)
    pallas_call x1, Pallas kernels, per_device(): pl.pallas_call(kernel, out_shape=(jax.ShapeDtypeStruct((WORK, CHIPS * COL...  158 us
    unnamed x11, local copies, waits for them, and re-layouts  8.81 us

profile of v1, /device:TPU:24, one launch (start us, length us, event | category | flops | bytes accessed | tf_op | source)
XLA Modules:
  0.0 169.1 jit_solution(10786519658400126054)
XLA Ops:
  0.6 1.4 copy.16.plan_ref
  2.0 1.4 copy.15.resp_ref
  3.4 158.2 %shard_map.129 = (bf16[144,12288]{1,0:T(8,128)(2,1)}, bf16[768,1024]{1,0:T(8,128)(2,1)}, f32[48,1024]{1,0:T(8,128)}, bf16[16,48,1024]{2,1,0:T(8,128)(2,1)}) custom-call(bf16[192,12288]{1,0:T(8,128)(2,1)} %x_hbm.1, bf16[192,1024]{1,0:T(8,128)(2,1)} %cot_hbm.1, bf16[768,1024]{1,0:T(8,128)(2,1)} %w_hbm.1, s32[192,1]{1,0:T(8,128)} %copy.15.resp_ref, ...), custom_call_target="tpu_custom_call" | custom-call | flops 8000000000 | bytes 20000000 | tf_op jit(solution)/shard_map/pallas_call | solution.py:316
  161.6 0.0 copy-start.1
  161.6 4.2 %copy.21 = bf16[144,12288]{1,0:T(8,128)(2,1)} copy(bf16[144,12288]{1,0:T(8,128)(2,1)} %get-tuple-element.16) | data formatting | bytes 7077888
  165.8 0.0 copy-done.1
  165.8 0.0 copy-start.2
  165.8 0.0 copy-start
  165.8 1.1 copy.22
  167.0 0.0 copy-done.2
  167.0 0.7 copy.23
  167.6 0.3 copy-done
  167.9 1.1 copy.24
Async XLA Ops:
  161.6 4.2 %copy-start.1 = (bf16[768,1024]{1,0:T(8,128)(2,1)S(1)}, bf16[768,1024]{1,0:T(8,128)(2,1)}, u32[]{:S(2)}) copy-start(bf16[768,1024]{1,0:T(8,128)(2,1)} %get-tuple-element.9) | copy-start | bytes 4718596
  165.8 1.1 copy-start.2
  165.8 2.1 %copy-start = (bf16[16,48,1024]{2,1,0:T(8,128)(2,1)S(1)}, bf16[16,48,1024]{2,1,0:T(8,128)(2,1)}, u32[]{:S(2)}) copy-start(bf16[16,48,1024]{2,1,0:T(8,128)(2,1)} %get-tuple-element.11) | copy-start | bytes 4718596

commit v2 on v1

--- a/solution.py
+++ b/solution.py
@@ -19,14 +19,16 @@
 COLS = 768
 PIECE = 48
 DEPTH = 8
+HALF = KV // 2
 
 GROUPS = (
     ((1, 0), (3, 0), (0, 1), (0, 3)),
     ((2, 0), (0, 2)),
     ((1, 1), (3, 3)),
     ((1, 3), (3, 1)),
+    ((2, 1), (2, 3)),
     ((2, 2),),
-    ((1, 2), (3, 2), (2, 1), (2, 3)),
+    ((1, 2), (3, 2)),
 )
 ALL = tuple(o for group in GROUPS for o in group)
 Z_ORDER = (4, 3, 5, 2, 6, 1, 7)
@@ -34,13 +36,19 @@
 
 def squash(e):
     sent, left = [], []
-    for j in range(KV // 128):
+    for j in range(e.shape[1] // 128):
         g = e[:, 128 * j : 128 * (j + 1)]
         m = jnp.mean(jnp.abs(g), axis=1, keepdims=True) + 1e-06
         s = (m * jnp.tanh(g * (1.0 / m))).astype(jnp.bfloat16)
         sent.append(s)
         left.append(g - s.astype(jnp.float32))
     return sent, left
+
+
+def upright(row):
+    n = row.shape[1]
+    here = lax.broadcasted_iota(jnp.int32, (n, n), 0) == lax.broadcasted_iota(jnp.int32, (n, n), 1)
+    return jnp.sum(jnp.where(here, row, 0), axis=1, keepdims=True)
 
 
 def row_weights(resp, rlen, grp, rew):
@@ -97,10 +105,10 @@
     for load in loads:
         load.start()
 
-    weight = row_weights(resp_ref[...], rlen_ref[...], grp_ref[...], rew_ref[...])
+    weight = row_weights(upright(resp_ref[...]), rlen_ref[...], grp_ref[...], rew_ref[...])
     goes = plan_ref[...]
-    target = jnp.where(goes[:, 0:1] >= 0, goes[:, 0:1] * (WORK // BLK) + goes[:, 2:3], -1)
-    pbuf[chip] = jnp.broadcast_to(target, (NBLK, 128))
+    target = jnp.where(goes[0:1] >= 0, goes[0:1] * (WORK // BLK) + goes[2:3], -1)
+    pbuf[chip] = jnp.broadcast_to(upright(target), (NBLK, 128))
     loads[0].wait()
     cbuf[y, x] = (weight * cot[...].astype(jnp.float32)).astype(jnp.bfloat16)
 
@@ -171,7 +179,7 @@
     for i in (8, 9, 10, 11):
         c[i].wait_recv()
         c[i + 4].start()
-    for o in GROUPS[3] + GROUPS[4] + GROUPS[5]:
+    for o in GROUPS[3] + GROUPS[4] + GROUPS[5] + GROUPS[6]:
         xs[o].start()
 
     for p in ps:
@@ -231,79 +239,142 @@
         g.start()
 
     loads[4].wait()
-    for o in ALL:
-        xs[o].wait_recv()
-    acc[...] = jnp.zeros_like(acc)
-
-    def contract(s, carry):
-        acc[...] += lax.dot_general(
-            xr[pl.ds(s * SIDE, SIDE)].reshape(SIDE * SLOT, COLS), cbuf[s].reshape(SIDE * SLOT, KV),
+    loads[2].wait()
+    loads[3].wait()
+
+    def contract(dy, cols):
+        s = lax.rem(y + SIDE - dy, SIDE)
+        part = lax.dot_general(
+            xr[pl.ds(s * SIDE, SIDE)].reshape(SIDE * SLOT, COLS),
+            cbuf[s, :, :, cols].reshape(SIDE * SLOT, cols.stop - cols.start),
             (((0,), (0,)), ((), ())), preferred_element_type=jnp.float32,
         )
-        return carry
-
-    lax.fori_loop(0, SIDE, contract, 0)
-
-    loads[2].wait()
-
-    def compress(which):
+        if dy == 0:
+            acc[:, cols] = part
+        else:
+            acc[:, cols] += part
+
+    for dy in (0, 1, 3, 2):
+        for dx in range(SIDE):
+            if (dx, dy) != (0, 0):
+                xs[dx, dy].wait_recv()
+        if dy != 2:
+            contract(dy, slice(0, KV))
+
+    def compress(which, h):
         def one(k, carry):
             p = pl.multiple_of((k * 2 + which) * PIECE, PIECE)
-            e = acc[pl.ds(p, PIECE), :] + serr[pl.ds(p, PIECE), :].astype(jnp.float32)
+            cols = slice(h * HALF, (h + 1) * HALF)
+            e = acc[pl.ds(p, PIECE), cols] + serr[pl.ds(p, PIECE), cols].astype(jnp.float32)
             sent, left = squash(e)
-            for j in range(KV // 128):
-                sbuf[which, k, :, 128 * j : 128 * (j + 1)] = sent[j]
-                nse_out[pl.ds(p, PIECE), 128 * j : 128 * (j + 1)] = left[j].astype(jnp.bfloat16)
+            for j in range(HALF // 128):
+                sbuf[h, which, k, :, 128 * j : 128 * (j + 1)] = sent[j]
+                at = h * HALF + 128 * j
+                nse_out[pl.ds(p, PIECE), at : at + 128] = left[j].astype(jnp.bfloat16)
             return carry
 
         lax.fori_loop(0, DEPTH, one, 0)
 
-    compress(other)
-    pair = remote(sbuf.at[other], sib, ssend, srecv, z * 2 + other, chip)
-    pair.start()
-    compress(core)
-    pair.wait_recv()
-
-    zc = {}
-    for dz in Z_ORDER:
-        to = deep(dz)
-        zs[to] = (sbuf[core, to].astype(jnp.float32) + sib[to].astype(jnp.float32)).astype(jnp.bfloat16)
-        zc[dz] = remote(zs.at[to], zr.at[dz], zsend.at[dz], zrecv.at[dz], to * 2 + core, chip)
-        zc[dz].start()
-    total = sbuf[core, z].astype(jnp.float32) + sib[z].astype(jnp.float32)
-    for dz in reversed(Z_ORDER):
-        zc[dz].wait_recv()
-        total = total + zr[dz].astype(jnp.float32)
-    loads[3].wait()
-    sent, left = squash(total * (1.0 / 16) + merr[...])
-    for j in range(KV // 128):
-        upd_out[node, :, 128 * j : 128 * (j + 1)] = sent[j]
-        nme_out[:, 128 * j : 128 * (j + 1)] = left[j]
-
-    us = {}
-    for dz in Z_ORDER:
-        us[dz] = remote(
-            upd_out.at[node], upd_out.at[node], usend.at[dz], urecv.at[dz], deep(dz) * 2 + core, chip
-        )
-        us[dz].start()
-    fs = []
-
-    def share(i, n):
-        f = remote(upd_out.at[n], upd_out.at[n], fsend.at[i], frecv.at[i], z * 2 + other, chip)
+    pair, zc = [], [{}, {}]
+    for h in (0, 1):
+        contract(2, slice(h * HALF, (h + 1) * HALF))
+        compress(other, h)
+        pair.append(remote(sbuf.at[h, other], sib.at[h], ssend.at[h], srecv.at[h], z * 2 + other, chip))
+        pair[h].start()
+        compress(core, h)
+        pair[h].wait_recv()
+        for dz in Z_ORDER:
+            to = deep(dz)
+            zs[h, to] = (
+                sbuf[h, core, to].astype(jnp.float32) + sib[h, to].astype(jnp.float32)
+            ).astype(jnp.bfloat16)
+            zc[h][dz] = remote(
+                zs.at[h, to], zr.at[h, dz], zsend.at[h, dz], zrecv.at[h, dz], to * 2 + core, chip
+            )
+            zc[h][dz].start()
+
+    sent_on = []
+
+    def ring(h, step, up):
+        n = deep(DEPTH - step if up else step) * 2 + core
+        cols = pl.ds(h * HALF, HALF)
+        if step == 3:
+            cols = pl.ds(h * HALF + (0 if up else HALF // 2), HALF // 2)
+        i = (h * 4 + step) * 2 + (1 if up else 0)
+        return remote(
+            upd_out.at[n, :, cols], upd_out.at[n, :, cols], usend.at[i], urecv.at[i],
+            deep(1 if up else DEPTH - 1) * 2 + core, chip,
+        )
+
+    def share(h, dz):
+        n = deep(dz) * 2 + core
+        block = upd_out.at[n, :, pl.ds(h * HALF, HALF)]
+        i = h * DEPTH + dz
+        f = remote(block, block, fsend.at[i], frecv.at[i], z * 2 + other, chip)
         f.start()
-        fs.append(f)
-
-    share(0, node)
-    for dz in reversed(Z_ORDER):
-        us[dz].wait_recv()
-        share(dz, deep(DEPTH - dz) * 2 + core)
+        return f
+
+    us, fs = {}, []
+
+    def average(h):
+        cols = slice(h * HALF, (h + 1) * HALF)
+        total = sbuf[h, core, z].astype(jnp.float32) + sib[h, z].astype(jnp.float32)
+        for dz in reversed(Z_ORDER):
+            zc[h][dz].wait_recv()
+            total = total + zr[h, dz].astype(jnp.float32)
+        sent, left = squash(total * (1.0 / 16) + merr[:, cols])
+        for j in range(HALF // 128):
+            at = h * HALF + 128 * j
+            upd_out[node, :, at : at + 128] = sent[j]
+            nme_out[:, at : at + 128] = left[j]
+        forward(h, 0)
+        fs.append(share(h, 0))
+
+    def forward(h, step):
+        for up in (True, False):
+            if step:
+                us[h, step - 1, up].wait_recv()
+            if step < 4:
+                us[h, step, up] = ring(h, step, up)
+                us[h, step, up].start()
+        if step in (1, 2, 3):
+            fs.append(share(h, DEPTH - step))
+            fs.append(share(h, step))
+        elif step == 4:
+            fs.append(share(h, 4))
+
+    average(0)
+    forward(0, 1)
+    average(1)
+    for step in (2, 3, 4):
+        forward(0, step)
+        forward(1, step - 1)
+    forward(1, 4)
     for f in fs:
         f.wait_recv()
     own_grad.wait()
     for g in gs:
         g.wait_recv()
-    for s in c + ps + gs + fs + [pair] + list(zc.values()) + list(us.values()):
+    for s in c + ps + gs + fs + pair + list(zc[0].values()) + list(zc[1].values()) + list(us.values()):
         s.wait_send()
+
+
+def leave(ig, nse, nme, upd, ig_out, nse_out, nme_out, upd_out, ig_v, nse_v, nme_v, upd_v, get, put):
+    parts = []
+    for src, mid, dst in ((ig, ig_v, ig_out), (nse, nse_v, nse_out), (upd, upd_v, upd_out), (nme, nme_v, nme_out)):
+        step = min(src.shape[0], 2 * PIECE)
+        for r in range(0, src.shape[0], step):
+            n = min(step, src.shape[0] - r)
+            parts.append([ref.at[pl.ds(r, n)] for ref in (src, mid, dst)])
+    reads = [pltpu.make_async_copy(a, b, get.at[i]) for i, (a, b, _) in enumerate(parts)]
+    writes = [pltpu.make_async_copy(b, c, put.at[i]) for i, (_, b, c) in enumerate(parts)]
+    for read in reads:
+        read.start()
+    for read, write in zip(reads, writes):
+        read.wait()
+        write.start()
+    for write in writes:
+        write.wait()
 
 
 def per_device(
@@ -334,27 +405,36 @@
             pltpu.VMEM((2 * WORK, KV), f32),
             pltpu.VMEM((CHIPS, WORK, COLS), bf16),
             pltpu.VMEM((COLS, KV), f32),
-            pltpu.VMEM((2, DEPTH, PIECE, KV), bf16),
-            pltpu.VMEM((DEPTH, PIECE, KV), bf16),
-            pltpu.VMEM((DEPTH, PIECE, KV), bf16),
-            pltpu.VMEM((DEPTH, PIECE, KV), bf16),
+            pltpu.VMEM((2, 2, DEPTH, PIECE, HALF), bf16),
+            pltpu.VMEM((2, DEPTH, PIECE, HALF), bf16),
+            pltpu.VMEM((2, DEPTH, PIECE, HALF), bf16),
+            pltpu.VMEM((2, DEPTH, PIECE, HALF), bf16),
             pltpu.VMEM((CHIPS, NBLK, 128), i32),
             pltpu.VMEM((1, 256), i32),
             pltpu.SMEM((1, 256), i32),
             dma((8,)), dma((16,)), dma((16,)), dma((16,)), dma((16,)), dma((16,)), dma((16,)),
-            dma((16,)), dma((16,)), dma, dma, dma((8,)), dma((8,)), dma((8,)), dma((8,)),
-            dma((8,)), dma((8,)),
+            dma((16,)), dma((16,)), dma((2,)), dma((2,)), dma((2, 8)), dma((2, 8)), dma((16,)), dma((16,)),
+            dma((16,)), dma((16,)),
         ],
         compiler_params=pltpu.CompilerParams(
             collective_id=0, has_side_effects=True, vmem_limit_bytes=58 * 2**20
         ),
         cost_estimate=pl.CostEstimate(flops=8_000_000_000, bytes_accessed=20_000_000, transcendentals=800_000),
     )(
-        x_rows, value_cot, value_weight, resp_of_row.reshape(SLOT, 1), block_plan,
+        x_rows, value_cot, value_weight, resp_of_row.reshape(1, SLOT), block_plan.T,
         resp_len.reshape(1, -1), group_of_resp.reshape(1, -1), rewards.reshape(1, -1),
         send_error.reshape(COLS, KV), mean_error.reshape(PIECE, KV),
     )
-    return ig, nse[None], nme[None, None], upd.reshape(COLS, KV)
+    upd = upd.reshape(COLS, KV)
+    ig, nse, nme, upd = pl.pallas_call(
+        leave,
+        out_shape=tuple(jax.ShapeDtypeStruct(a.shape, a.dtype) for a in (ig, nse, nme, upd)),
+        in_specs=[hbm] * 4,
+        out_specs=[hbm] * 4,
+        scratch_shapes=[pltpu.VMEM(a.shape, a.dtype) for a in (ig, nse, nme, upd)] + [dma((24,)), dma((24,))],
+        compiler_params=pltpu.CompilerParams(vmem_limit_bytes=58 * 2**20),
+    )(ig, nse, nme, upd)
+    return ig, nse[None], nme[None, None], upd
 
 
 def solution(mesh):

time: 171 us -> 157 us (0.918)
  local copies, waits for them, and re-layouts: 10.2 us -> 0 us
  Pallas kernels: 158 us -> 155 us
    unnamed x11 -> x0, local copies, waits for them, and re-layouts: 8.81 us -> none
    pallas_call x1, Pallas kernels: 158 us -> 150 us  [per_device(): pl.pallas_call(kernel, out_shape=(jax.ShapeDtypeStruct((WORK, CHIPS * COL...]
    pallas_call x0 -> x1, Pallas kernels: none -> 4.95 us  [per_device(): pl.pallas_call(leave, out_shape=tuple((jax.ShapeDtypeStruct(a.shape, a.dt...]
where the time goes in v2:
time: 157 us; the launch traced here: 155 us
  Pallas kernels  155 us (99%)
    pallas_call x1, Pallas kernels, per_device(): pl.pallas_call(kernel, out_shape=(jax.ShapeDtypeStruct((WORK, CHIPS * COL...  150 us
    pallas_call x1, Pallas kernels, per_device(): pl.pallas_call(leave, out_shape=tuple((jax.ShapeDtypeStruct(a.shape, a.dt...  4.95 us

profile of v2, /device:TPU:24, one launch (start us, length us, event | category | flops | bytes accessed | tf_op | source)
XLA Modules:
  0.0 155.3 jit_solution(11645891777505023359)
XLA Ops:
  0.6 149.7 %shard_map.129 = (bf16[144,12288]{1,0:T(8,128)(2,1)}, bf16[768,1024]{1,0:T(8,128)(2,1)}, f32[48,1024]{1,0:T(8,128)}, bf16[16,48,1024]{2,1,0:T(8,128)(2,1)}) custom-call(bf16[192,12288]{1,0:T(8,128)(2,1)} %x_hbm.1, bf16[192,1024]{1,0:T(8,128)(2,1)} %cot_hbm.1, bf16[768,1024]{1,0:T(8,128)(2,1)} %w_hbm.1, s32[1,192]{1,0:T(1,128)} %bitcast.19, ...), custom_call_target="tpu_custom_call" | custom-call | flops 8000000000 | bytes 20000000 | tf_op jit(solution)/shard_map/pallas_call | solution.py:387
  150.3 4.9 %shard_map.130 = (bf16[144,12288]{1,0:T(8,128)(2,1)}, bf16[768,1024]{1,0:T(8,128)(2,1)}, f32[48,1024]{1,0:T(8,128)}, bf16[768,1024]{1,0:T(8,128)(2,1)}) custom-call(bf16[144,12288]{1,0:T(8,128)(2,1)} %get-tuple-element.12.ig, bf16[768,1024]{1,0:T(8,128)(2,1)} %get-tuple-element.13.nse, f32[48,1024]{1,0:T(8,128)} %get-tuple-element.14.nme, ...), custom_call_target="tpu_custom_call" | custom-call | tf_op jit(solution)/shard_map/pallas_call | solution.py:429

commit v3 on v2

--- a/solution.py
+++ b/solution.py
@@ -161,7 +161,7 @@
         c[i].start()
     for p in ps:
         p.start()
-    for o in GROUPS[0]:
+    for o in GROUPS[0] + GROUPS[1] + GROUPS[2]:
         xs[o].start()
     for i in (0, 1, 2, 3):
         c[i].wait_recv()
@@ -174,12 +174,12 @@
         c[i].wait_recv()
     c[10].start()
     c[11].start()
-    for o in GROUPS[1] + GROUPS[2]:
+    for o in GROUPS[3] + GROUPS[4]:
         xs[o].start()
     for i in (8, 9, 10, 11):
         c[i].wait_recv()
         c[i + 4].start()
-    for o in GROUPS[3] + GROUPS[4] + GROUPS[5] + GROUPS[6]:
+    for o in GROUPS[5] + GROUPS[6]:
         xs[o].start()
 
     for p in ps:
@@ -228,6 +228,29 @@
             gsend.at[i], grecv.at[i], node, to,
         )
 
+    loads[4].wait()
+
+    def contract(dy, cols):
+        s = lax.rem(y + SIDE - dy, SIDE)
+        part = lax.dot_general(
+            xr[pl.ds(s * SIDE, SIDE)].reshape(SIDE * SLOT, COLS),
+            cbuf[s, :, :, cols].reshape(SIDE * SLOT, cols.stop - cols.start),
+            (((0,), (0,)), ((), ())), preferred_element_type=jnp.float32,
+        )
+        if dy == 0:
+            acc[:, cols] = part
+        else:
+            acc[:, cols] += part
+
+    def arrived(dy):
+        for dx in range(SIDE):
+            if (dx, dy) != (0, 0):
+                xs[dx, dy].wait_recv()
+
+    for dy in (0, 1, 3):
+        arrived(dy)
+        contract(dy, slice(0, KV))
+
     own_grad = pltpu.make_async_copy(
         gbuf.at[chip], ig_out.at[:, pl.ds(pl.multiple_of(chip * COLS, 128), COLS)], lsem.at[6]
     )
@@ -237,29 +260,6 @@
     gs = [owners(*o) for o in ALL]
     for g in gs:
         g.start()
-
-    loads[4].wait()
-    loads[2].wait()
-    loads[3].wait()
-
-    def contract(dy, cols):
-        s = lax.rem(y + SIDE - dy, SIDE)
-        part = lax.dot_general(
-            xr[pl.ds(s * SIDE, SIDE)].reshape(SIDE * SLOT, COLS),
-            cbuf[s, :, :, cols].reshape(SIDE * SLOT, cols.stop - cols.start),
-            (((0,), (0,)), ((), ())), preferred_element_type=jnp.float32,
-        )
-        if dy == 0:
-            acc[:, cols] = part
-        else:
-            acc[:, cols] += part
-
-    for dy in (0, 1, 3, 2):
-        for dx in range(SIDE):
-            if (dx, dy) != (0, 0):
-                xs[dx, dy].wait_recv()
-        if dy != 2:
-            contract(dy, slice(0, KV))
 
     def compress(which, h):
         def one(k, carry):
@@ -275,6 +275,9 @@
 
         lax.fori_loop(0, DEPTH, one, 0)
 
+    loads[2].wait()
+    loads[3].wait()
+    arrived(2)
     pair, zc = [], [{}, {}]
     for h in (0, 1):
         contract(2, slice(h * HALF, (h + 1) * HALF))

time: 157 us -> 155 us (0.987)
  Pallas kernels: 155 us -> 152 us
    pallas_call x1, Pallas kernels: 150 us -> 147 us  [per_device(): pl.pallas_call(kernel, out_shape=(jax.ShapeDtypeStruct((WORK, CHIPS * COL...]
where the time goes in v3:
time: 155 us; the launch traced here: 153 us
  Pallas kernels  152 us (98%)
    pallas_call x1, Pallas kernels, per_device(): pl.pallas_call(kernel, out_shape=(jax.ShapeDtypeStruct((WORK, CHIPS * COL...  147 us
    pallas_call x1, Pallas kernels, per_device(): pl.pallas_call(leave, out_shape=tuple((jax.ShapeDtypeStruct(a.shape, a.dt...  4.95 us

profile of v3, /device:TPU:24, one launch (start us, length us, event | category | flops | bytes accessed | tf_op | source)
XLA Modules:
  0.0 152.7 jit_solution(5248532283703138891)
XLA Ops:
  0.6 147.1 %shard_map.129 = (bf16[144,12288]{1,0:T(8,128)(2,1)}, bf16[768,1024]{1,0:T(8,128)(2,1)}, f32[48,1024]{1,0:T(8,128)}, bf16[16,48,1024]{2,1,0:T(8,128)(2,1)}) custom-call(bf16[192,12288]{1,0:T(8,128)(2,1)} %x_hbm.1, bf16[192,1024]{1,0:T(8,128)(2,1)} %cot_hbm.1, bf16[768,1024]{1,0:T(8,128)(2,1)} %w_hbm.1, s32[1,192]{1,0:T(1,128)} %bitcast.19, ...), custom_call_target="tpu_custom_call" | custom-call | flops 8000000000 | bytes 20000000 | tf_op jit(solution)/shard_map/pallas_call | solution.py:390
  147.7 4.9 %shard_map.130 = (bf16[144,12288]{1,0:T(8,128)(2,1)}, bf16[768,1024]{1,0:T(8,128)(2,1)}, f32[48,1024]{1,0:T(8,128)}, bf16[768,1024]{1,0:T(8,128)(2,1)}) custom-call(bf16[144,12288]{1,0:T(8,128)(2,1)} %get-tuple-element.12.ig, bf16[768,1024]{1,0:T(8,128)(2,1)} %get-tuple-element.13.nse, f32[48,1024]{1,0:T(8,128)} %get-tuple-element.14.nme, ...), custom_call_target="tpu_custom_call" | custom-call | tf_op jit(solution)/shard_map/pallas_call | solution.py:432

commit v4 on v3

--- a/solution.py
+++ b/solution.py
@@ -161,7 +161,7 @@
         c[i].start()
     for p in ps:
         p.start()
-    for o in GROUPS[0] + GROUPS[1] + GROUPS[2]:
+    for o in GROUPS[0] + GROUPS[1] + GROUPS[2] + GROUPS[3]:
         xs[o].start()
     for i in (0, 1, 2, 3):
         c[i].wait_recv()
@@ -174,12 +174,12 @@
         c[i].wait_recv()
     c[10].start()
     c[11].start()
-    for o in GROUPS[3] + GROUPS[4]:
+    for o in GROUPS[4] + GROUPS[5]:
         xs[o].start()
     for i in (8, 9, 10, 11):
         c[i].wait_recv()
         c[i + 4].start()
-    for o in GROUPS[5] + GROUPS[6]:
+    for o in GROUPS[6]:
         xs[o].start()
 
     for p in ps:

time: 155 us -> 158 us (1.019); the launches traced: 153 us -> 158 us
  Pallas kernels: 152 us -> 157 us
    pallas_call x1, Pallas kernels: 147 us -> 152 us  [per_device(): pl.pallas_call(kernel, out_shape=(jax.ShapeDtypeStruct((WORK, CHIPS * COL...]
where the time goes in v4:
time: 158 us
  Pallas kernels  157 us (99%)
    pallas_call x1, Pallas kernels, per_device(): pl.pallas_call(kernel, out_shape=(jax.ShapeDtypeStruct((WORK, CHIPS * COL...  152 us
    pallas_call x1, Pallas kernels, per_device(): pl.pallas_call(leave, out_shape=tuple((jax.ShapeDtypeStruct(a.shape, a.dt...  4.95 us

profile of v4, /device:TPU:24, one launch (start us, length us, event | category | flops | bytes accessed | tf_op | source)
XLA Modules:
  0.0 157.8 jit_solution(12524798778748462999)
XLA Ops:
  0.6 152.2 %shard_map.129 = (bf16[144,12288]{1,0:T(8,128)(2,1)}, bf16[768,1024]{1,0:T(8,128)(2,1)}, f32[48,1024]{1,0:T(8,128)}, bf16[16,48,1024]{2,1,0:T(8,128)(2,1)}) custom-call(bf16[192,12288]{1,0:T(8,128)(2,1)} %x_hbm.1, bf16[192,1024]{1,0:T(8,128)(2,1)} %cot_hbm.1, bf16[768,1024]{1,0:T(8,128)(2,1)} %w_hbm.1, s32[1,192]{1,0:T(1,128)} %bitcast.19, ...), custom_call_target="tpu_custom_call" | custom-call | flops 8000000000 | bytes 20000000 | tf_op jit(solution)/shard_map/pallas_call | solution.py:390
  152.8 4.9 %shard_map.130 = (bf16[144,12288]{1,0:T(8,128)(2,1)}, bf16[768,1024]{1,0:T(8,128)(2,1)}, f32[48,1024]{1,0:T(8,128)}, bf16[768,1024]{1,0:T(8,128)(2,1)}) custom-call(bf16[144,12288]{1,0:T(8,128)(2,1)} %get-tuple-element.12.ig, bf16[768,1024]{1,0:T(8,128)(2,1)} %get-tuple-element.13.nse, f32[48,1024]{1,0:T(8,128)} %get-tuple-element.14.nme, ...), custom_call_target="tpu_custom_call" | custom-call | tf_op jit(solution)/shard_map/pallas_call | solution.py:432
